TPU v7x, 32 devices: a whole 2x2x4 slice. The times are simulated.
32 devices in a mesh: groups: 2 (over x), img: 16 (over z, y, core).
Axes of the slice: x: 2, y: 2, z: 4, core: 2. Of those that a mesh axis runs over, the one named last changes fastest.
Arguments:
- tokens: bfloat16 [256, 196, 768], P(('groups', 'img')), parts along dimension 0, may hold values from -60 to 60
- pair_list: int32 [256, 2], P(('groups', 'img')), parts along dimension 0, may hold values from 0 to 127, as said below
- w_query: bfloat16 [768, 768], replicated, may hold values from -1.5 to 1.5
- w_key: bfloat16 [768, 768], replicated, may hold values from -1.5 to 1.5
- w_value: bfloat16 [768, 768], replicated, may hold values from -0.21875 to 0.21875
- w_out: bfloat16 [768, 768], replicated, may hold values from -0.21875 to 0.21875
- gain_query: float32 [768], replicated, may hold values from 0.1 to 1.9
- context_norm_gain: float32 [768], replicated, may hold values from 0.1 to 1.9
- conf_weight: float32 [768], replicated, may hold values from -0.21875 to 0.21875
Outputs:
- merged: float32 [256, 196, 768], P(('groups', 'img')), parts along dimension 0
There are 2 independent parts, one for each index of `groups`. A program takes and returns all parts, laid end to end along the dimension named above; an argument that names none is the same for every part. Nothing has to cross between parts.
Inputs may be any that keep to these rules, and one draw needn't show every extreme that they name: Image i is held by device i // 8 of img, and row r of pair_list is listed at device r // 8, which holds the pair's first image. The second image differs from the first. Among the 8 rows of one device at most 1 name a second image held by any one device, and in every draw some device holds the second images of exactly 1 row of every device.
All inputs are finite; a program needn't handle non-finite values.
Results may differ from a plain program's by a relative error of at most 0.0009.
Values may be sent and summed in bfloat16 or wider, within the bound.
No kernel may reach another device: no remote copies, remote signals or barrier semaphores. Data moves between devices by JAX's collectives and lax.ppermute only.
A program may use at most 192 MiB of HBM per device.

v0:
```python
import functools
import math

import jax
import jax.numpy as jnp
from jax import lax
from jax.experimental import pallas as pl
from jax.experimental.pallas import tpu as pltpu
from jax.sharding import PartitionSpec as P

HEADS = 12
EPSILON = 1e-06
SLOTS = 2
PLANE = 4
VMEM = pl.BlockSpec(memory_space=pltpu.VMEM)
SMEM = pl.BlockSpec(memory_space=pltpu.SMEM)
ANY = pl.BlockSpec(memory_space=pl.ANY)
LIMIT = 56 * 1024 * 1024


def round_up(value, step):
    return (value + step - 1) // step * step


def image_at(ref, image, rows):
    if len(ref.shape) == 3:
        return ref.at[image]
    return ref.at[pl.ds(pl.multiple_of(image * rows, 8), rows)]


def centred_scaled(values):
    widened = values.astype(jnp.float32)
    centre = jnp.mean(widened, axis=-1, keepdims=True)
    shifted = widened - centre
    spread = jnp.mean(jnp.square(shifted), axis=-1, keepdims=True)
    return shifted * lax.rsqrt(spread + EPSILON)


def prep_kernel(tokens_ref, wq_t_ref, gain_ref, conf_row_ref, q_t_ref, conf_ref, normed):
    images, length, _ = tokens_ref.shape
    lanes = q_t_ref.shape[2]
    scale = 1.0 / math.sqrt(tokens_ref.shape[2] // HEADS)
    normed[...] = jnp.zeros_like(normed)
    diagonal = lax.broadcasted_iota(jnp.int32, (length, lanes), 0) == lax.broadcasted_iota(
        jnp.int32, (length, lanes), 1
    )

    def one_image(image, carry):
        own = tokens_ref[image]
        normed[0:length, :] = (centred_scaled(own) * gain_ref[...]).astype(jnp.bfloat16)
        queries = lax.dot_general(
            wq_t_ref[...],
            normed[...],
            (((1,), (1,)), ((), ())),
            preferred_element_type=jnp.float32,
        ).astype(jnp.bfloat16)
        q_t_ref[image] = queries * jnp.asarray(scale, jnp.bfloat16)
        sums = jnp.sum(own.astype(jnp.float32) * conf_row_ref[...], axis=-1, keepdims=True)
        conf_ref[image] = jnp.sum(jnp.where(diagonal, sums, 0.0), axis=0, keepdims=True)
        return carry

    lax.fori_loop(0, images, one_image, 0)


def image_is_needed(firsts_ref, seconds_ref, devices, asker, owner, slot):
    if slot == 0:
        spot = asker * devices + owner
        return seconds_ref[spot] - 1, firsts_ref[spot] - 1
    spot = owner * devices + asker
    return firsts_ref[spot] - 1, seconds_ref[spot] - 1


def branch_kernel(
    plan,
    devices,
    sources,
    first_call,
    last_call,
    firsts_ref,
    seconds_ref,
    me_ref,
    *refs,
):
    partner_refs = refs[:sources]
    rest = list(refs[sources:])
    tok_conf_ref, gain_ref, conf_col_ref = rest[:3]
    stored = rest[3:7]
    rest = rest[7:]
    if not first_call:
        denom_in, numer_in = rest[:2]
        rest = rest[2:]
    if last_call:
        tokens_in, merged_ref = rest[:2]
        numer, denom, tokens_ref = rest[2:5]
        rest = rest[5:]
    else:
        numer, denom = rest[:2]
        rest = rest[2:]
    q_t_ref, wk_ref, wv_t_ref, wo_t_ref = loaded = rest[:4]
    listed, whole_arrived, arrived, normed, keys, values_t, scores, probs, mixed_t = rest[4:13]
    copy_sem, load_sem = rest[13:]
    loads = [
        pltpu.make_async_copy(origin, target, load_sem.at[turn])
        for turn, (origin, target) in enumerate(zip(stored, loaded))
    ]
    if not first_call:
        loads.append(pltpu.make_async_copy(numer_in, numer, load_sem.at[4]))
    for turn in (1, 2, 0, 3, 4):
        if turn < len(loads):
            loads[turn].start()
    if last_call:
        tokens_load = pltpu.make_async_copy(tokens_in, tokens_ref, load_sem.at[5])
        tokens_load.start()
    images, feats, lanes = q_t_ref.shape
    length, rows = whole_arrived.shape[1], arrived.shape[1]
    key_rows = keys.shape[0]
    head_dim = feats // HEADS
    whole = length // 16 * 16
    me = me_ref[0]

    total = jnp.int32(0)
    for buffer_of, owner_of, slot, taken_of in plan:
        owner = owner_of(me)
        wanted, own = image_is_needed(firsts_ref, seconds_ref, devices, me, owner, slot)
        valid = (wanted >= 0) & taken_of(me)
        buffer, spot = buffer_of(me, wanted)

        @pl.when(valid)
        def _(total=total, buffer=buffer, spot=spot, own=own):
            listed[total, 0] = buffer
            listed[total, 1] = spot
            listed[total, 2] = own

        total = total + valid.astype(jnp.int32)

    def copies(turn, act):
        slot = turn % 2
        for source, ref in enumerate(partner_refs):

            @pl.when(listed[turn, 0] == source)
            def _(ref=ref):
                landing = whole_arrived if len(ref.shape) == 3 else arrived
                act(
                    pltpu.make_async_copy(
                        image_at(ref, listed[turn, 1], rows), landing.at[slot], copy_sem.at[slot]
                    )
                )
                if act is finish and len(ref.shape) == 3:
                    arrived[slot, 0:length, :] = whole_arrived[slot]

    def begin(copy):
        copy.start()

    def finish(copy):
        copy.wait()

    def fetch(turn):
        copies(turn, begin)

    @pl.when(total > 0)
    def _():
        fetch(0)

    normed[...] = jnp.zeros_like(normed)
    probs[:, key_rows:, :] = jnp.zeros((HEADS, lanes - key_rows, lanes), jnp.bfloat16)
    if first_call:
        numer[...] = jnp.zeros_like(numer)
        denom[...] = jnp.ones_like(denom)
    else:
        denom[...] = denom_in[...]

    tail_rows = lax.broadcasted_iota(jnp.int32, (key_rows - whole, 128), 0) + whole
    tail_ok = tail_rows < length

    def one_branch(turn, carry):
        slot = turn % 2
        copies(turn, finish)

        @pl.when(turn + 1 < total)
        def _():
            fetch(turn + 1)

        image = listed[turn, 2]

        def loaded_by_now(which):
            @pl.when(turn == 0)
            def _():
                loads[which].wait()

        normed[0:length, :] = (centred_scaled(arrived[slot, 0:length, :]) * gain_ref[...]).astype(jnp.bfloat16)
        loaded_by_now(1)
        keys[...] = jnp.dot(
            normed[0:key_rows, :], wk_ref[...], preferred_element_type=jnp.float32
        ).astype(jnp.bfloat16)
        loaded_by_now(2)
        values_t[...] = lax.dot_general(
            wv_t_ref[...],
            normed[...],
            (((1,), (1,)), ((), ())),
            preferred_element_type=jnp.float32,
        ).astype(jnp.bfloat16)
        zero_rows = jnp.zeros((head_dim, lanes), jnp.bfloat16)
        loaded_by_now(0)
        for head in range(HEADS):
            own_q = q_t_ref[image, head * head_dim : (head + 1) * head_dim, :]
            pair = head // 2
            ordered = [own_q, zero_rows] if head % 2 == 0 else [zero_rows, own_q]
            scores[head] = jnp.dot(
                keys[:, pair * 2 * head_dim : (pair + 1) * 2 * head_dim],
                jnp.concatenate(ordered, axis=0),
                preferred_element_type=jnp.float32,
            )
        for head in range(HEADS):
            for part in range(0, lanes, 128):
                body = scores[head, 0:whole, part : part + 128]
                tail = jnp.where(
                    tail_ok, scores[head, whole:key_rows, part : part + 128], -jnp.inf
                )
                top = jnp.maximum(
                    jnp.max(body, axis=0, keepdims=True), jnp.max(tail, axis=0, keepdims=True)
                )
                body = jnp.exp(body - top)
                tail = jnp.exp(tail - top)
                share = 1.0 / (
                    jnp.sum(body, axis=0, keepdims=True) + jnp.sum(tail, axis=0, keepdims=True)
                )
                probs[head, 0:whole, part : part + 128] = (body * share).astype(jnp.bfloat16)
                probs[head, whole:key_rows, part : part + 128] = (tail * share).astype(
                    jnp.bfloat16
                )
        for head in range(HEADS):
            part = slice(head * head_dim, (head + 1) * head_dim)
            mixed_t[part, :] = jnp.dot(
                values_t[part, :], probs[head], preferred_element_type=jnp.float32
            ).astype(jnp.bfloat16)
        loaded_by_now(3)
        update = (
            jnp.dot(wo_t_ref[...], mixed_t[...], preferred_element_type=jnp.float32)
            .astype(jnp.bfloat16)
            .astype(jnp.float32)
        )
        logit = tok_conf_ref[image] + jnp.concatenate(
            [
                jnp.sum(update[:, part : part + 128] * conf_col_ref[...], axis=0, keepdims=True)
                for part in range(0, lanes, 128)
            ],
            axis=1,
        )
        conf = 1.0 + jnp.maximum(logit, 0.0) + jnp.log1p(jnp.exp(-jnp.abs(logit)))
        if not first_call:
            loaded_by_now(4)
        numer[image] += conf * update
        denom[image] += conf
        return carry

    lax.fori_loop(0, total, one_branch, 0)

    @pl.when(total == 0)
    def _():
        for load in loads:
            load.wait()

    if last_call:
        tokens_load.wait()
        for image in range(images):
            ratio = jnp.transpose(numer[image] * (1.0 / denom[image]))
            merged = tokens_ref[image].astype(jnp.float32) + ratio[0:length, :]
            for part in range(feats // 128):
                merged_ref[
                    pl.ds(part * images + image, length, stride=feats // 128 * images), :
                ] = merged[:, part * 128 : (part + 1) * 128]


def pack_kernel(plan, devices, sources, firsts_ref, seconds_ref, me_ref, *refs):
    source_refs = refs[:sources]
    whole_staged, staged, in_sem, out_sem = refs[-4:]
    out_refs = refs[sources:-4]
    me = me_ref[0]
    length, rows = whole_staged.shape[1], staged.shape[1]
    jobs = []
    for spot, (buffer_of, owner_of, asker_of, slot, taken_of, out, place) in enumerate(plan):
        wanted, _ = image_is_needed(
            firsts_ref, seconds_ref, devices, asker_of(me), owner_of(me), slot
        )
        valid = (wanted >= 0) & taken_of(me)
        buffer, origin = buffer_of(me, wanted)
        for source, ref in enumerate(source_refs):
            landing = whole_staged if len(ref.shape) == 3 else staged
            jobs.append(
                (
                    spot,
                    valid & (buffer == source),
                    image_at(ref, origin, rows),
                    landing,
                    out_refs[out].at[pl.ds(place * rows, rows)],
                )
            )
    for spot, valid, origin, landing, _ in jobs:

        @pl.when(valid)
        def _(spot=spot, origin=origin, landing=landing):
            pltpu.make_async_copy(origin, landing.at[spot], in_sem.at[spot]).start()

    for spot, valid, origin, landing, target in jobs:

        @pl.when(valid)
        def _(spot=spot, origin=origin, landing=landing, target=target):
            pltpu.make_async_copy(origin, landing.at[spot], in_sem.at[spot]).wait()
            if landing is whole_staged:
                staged[spot, 0:length, :] = whole_staged[spot]
            pltpu.make_async_copy(staged.at[spot], target, out_sem.at[spot]).start()

    for spot, valid, _, _, target in jobs:

        @pl.when(valid)
        def _(spot=spot, target=target):
            pltpu.make_async_copy(staged.at[spot], target, out_sem.at[spot]).wait()


def pack(plan, tables, devices, length, sources, outs, places):
    rows, feats = round_up(length, 8), sources[0].shape[-1]
    return pl.pallas_call(
        functools.partial(pack_kernel, plan, devices, len(sources)),
        out_shape=tuple(
            jax.ShapeDtypeStruct((places * rows, feats), jnp.bfloat16) for _ in range(outs)
        ),
        in_specs=[SMEM] * 3 + [ANY] * len(sources),
        out_specs=(ANY,) * outs,
        scratch_shapes=[
            pltpu.VMEM((len(plan), length, feats), jnp.bfloat16),
            pltpu.VMEM((len(plan), rows, feats), jnp.bfloat16),
            pltpu.SemaphoreType.DMA((len(plan),)),
            pltpu.SemaphoreType.DMA((len(plan),)),
        ],
        compiler_params=pltpu.CompilerParams(vmem_limit_bytes=LIMIT),
        name="pack_images",
    )(*tables, *sources)


def run_branches(plan, tables, devices, length, partners, shared, sums, tokens=None):
    images, feats, lanes = shared[3].shape
    last_call = tokens is not None
    kept = (
        jax.ShapeDtypeStruct((images, feats, lanes), jnp.float32),
        jax.ShapeDtypeStruct((images, 1, lanes), jnp.float32),
    )
    operands = [*tables, *partners, *shared]
    specs = [SMEM] * 3 + [ANY] * len(partners) + [VMEM] * 3 + [ANY] * 4
    if sums is not None:
        operands += [sums[1], sums[0]]
        specs += [VMEM, ANY]
    scratch = []
    if last_call:
        operands.append(tokens)
        specs.append(ANY)
        outs = jax.ShapeDtypeStruct((length * images * feats // 128, 128), jnp.float32)
        out_specs = VMEM
        scratch = [pltpu.VMEM(k.shape, k.dtype) for k in (*kept, tokens)]
    else:
        outs, out_specs = kept, (VMEM, VMEM)
    key_rows = round_up(length, 16)
    scratch += [pltpu.VMEM(k.shape, k.dtype) for k in shared[3:]]
    scratch += [
        pltpu.SMEM((len(plan), 3), jnp.int32),
        pltpu.VMEM((2, length, feats), jnp.bfloat16),
        pltpu.VMEM((2, round_up(length, 8), feats), jnp.bfloat16),
        pltpu.VMEM((lanes, feats), jnp.bfloat16),
        pltpu.VMEM((key_rows, feats), jnp.bfloat16),
        pltpu.VMEM((feats, lanes), jnp.bfloat16),
        pltpu.VMEM((HEADS, key_rows, lanes), jnp.float32),
        pltpu.VMEM((HEADS, lanes, lanes), jnp.bfloat16),
        pltpu.VMEM((feats, lanes), jnp.bfloat16),
        pltpu.SemaphoreType.DMA((2,)),
        pltpu.SemaphoreType.DMA((6,)),
    ]
    expected = max(len(plan) // 2, 1)
    return pl.pallas_call(
        functools.partial(
            branch_kernel, plan, devices, len(partners), sums is None, last_call
        ),
        out_shape=outs,
        in_specs=specs,
        out_specs=out_specs,
        scratch_shapes=scratch,
        compiler_params=pltpu.CompilerParams(vmem_limit_bytes=LIMIT),
        cost_estimate=pl.CostEstimate(
            flops=expected * 1300000000, bytes_accessed=expected * 2000000, transcendentals=0
        ),
        name="attend_branches",
    )(*operands)


def prepare(tokens, wq_t, gain_query, conf_weight):
    images, length, feats = tokens.shape
    lanes = round_up(length, 128)
    return pl.pallas_call(
        prep_kernel,
        out_shape=(
            jax.ShapeDtypeStruct((images, feats, lanes), jnp.bfloat16),
            jax.ShapeDtypeStruct((images, 1, lanes), jnp.float32),
        ),
        in_specs=[VMEM] * 4,
        out_specs=(VMEM, VMEM),
        scratch_shapes=[pltpu.VMEM((lanes, feats), jnp.bfloat16)],
        compiler_params=pltpu.CompilerParams(vmem_limit_bytes=LIMIT),
        name="own_queries",
    )(tokens, wq_t, gain_query[None, :], conf_weight[None, :])


def pair_tables(pair_list, per_device, devices):
    pairs = lax.all_gather(pair_list, "img", axis=0, tiled=False)
    listing = jnp.arange(devices, dtype=jnp.int32)
    first_local = pairs[:, :, 0] - listing[:, None] * per_device
    owner = pairs[:, :, 1] // per_device
    second_local = pairs[:, :, 1] - owner * per_device
    hit = owner[:, :, None] == listing[None, None, :]
    firsts = jnp.sum(jnp.where(hit, first_local[:, :, None] + 1, 0), axis=1)
    seconds = jnp.sum(jnp.where(hit, second_local[:, :, None] + 1, 0), axis=1)
    return firsts, seconds


def always(me):
    return jnp.bool_(True)


def own_image(me, wanted):
    return 0, wanted


def fixed(buffer, spot):
    return lambda me, wanted: (buffer, spot)


def dense_exchange(tokens, tables, devices, shared):
    length = tokens.shape[1]
    places = [(other, slot) for other in range(devices) for slot in range(SLOTS)]
    packing = [
        (own_image, lambda me: me, lambda me, other=other: other, slot, always, 0, spot)
        for spot, (other, slot) in enumerate(places)
    ]
    (packed,) = pack(packing, tables, devices, length, (tokens,), 1, len(places))
    fetched = lax.all_to_all(packed, "img", split_axis=0, concat_axis=0, tiled=True)
    branches = [
        (fixed(0, spot), lambda me, other=other: other, slot, always)
        for spot, (other, slot) in enumerate(places)
    ]
    return run_branches(branches, tables, devices, length, (fetched,), shared, None, tokens)


def line_exchange(tokens, tables, devices, shared_of):
    length = tokens.shape[1]
    changes = range(1, PLANE)
    slots = range(SLOTS)
    pinned = lax.optimization_barrier

    def hop(array, step, origins):
        return lax.ppermute(
            array,
            "img",
            [(p * PLANE + c, (p + step) * PLANE + c) for p in origins for c in range(PLANE)],
        )

    def across(array, flip, change, planes=range(4)):
        return lax.ppermute(
            array,
            "img",
            [
                (p * PLANE + c, (p ^ flip) * PLANE + (c ^ change))
                for p in planes
                for c in range(PLANE)
            ],
        )

    def other(flip, change):
        return lambda me: ((me // PLANE) ^ flip) * PLANE + ((me % PLANE) ^ change)

    def same(me):
        return me

    def hopped(flip, base):
        return lambda me, wanted: (
            base + jnp.where((me // PLANE) ^ flip > me // PLANE, 1, 0),
            wanted,
        )

    def inner(me):
        plane = me // PLANE
        return (plane == 1) | (plane == 2)

    def outer(me):
        return jnp.logical_not(inner(me))

    def pack_for(packing, sources, outs):
        return pack(packing, tables, devices, length, sources, outs, SLOTS)

    def to_others(packed):
        return [across(packed[change - 1], 0, change) for change in changes]

    tokens, *tables = pinned((tokens, *tables))
    up_one = hop(tokens, 1, (0, 1, 2))
    down_one = hop(tokens, -1, (1, 2, 3))
    packing = [
        (own_image, same, other(0, change), slot, always, change - 1, slot)
        for change in changes
        for slot in slots
    ]
    within = to_others(pack_for(packing, (tokens,), PLANE - 1))
    shared = shared_of()
    up_one, down_one, within, shared = pinned((up_one, down_one, within, shared))

    up_two = hop(up_one, 1, (1, 2))
    down_two = hop(down_one, -1, (1, 2))
    packing = [
        entry
        for change in changes
        for slot in slots
        for entry in (
            (own_image, same, other(3, change), slot, outer, change - 1, slot),
            (hopped(3, 1), other(3, 0), other(0, change), slot, inner, change - 1, slot),
            (hopped(1, 1), other(1, 0), other(0, change), slot, always, change + PLANE - 2, slot),
        )
    ]
    packed = pack_for(packing, (tokens, up_one, down_one), 2 * (PLANE - 1))
    cross = to_others(packed[: PLANE - 1])
    shared, packed = pinned((shared, packed))
    branches = [
        (own_image if change == 0 else fixed(change, slot), other(0, change), slot, always)
        for change in range(PLANE)
        for slot in slots
    ]
    sums = run_branches(branches, tables, devices, length, (tokens, *within), shared, None)
    packed, cross, sums = pinned((packed, cross, sums))
    near = to_others(packed[PLANE - 1 :])
    packing = [
        (
            own_image if change == 0 else fixed(change, slot),
            other(0, change),
            other(3, 0),
            slot,
            outer,
            change // 2,
            change % 2 * SLOTS + slot,
        )
        for change in range(PLANE)
        for slot in slots
    ]
    ends = pack(packing, tables, devices, length, (tokens, *cross), 2, 2 * SLOTS)
    up_two, down_two, ends = pinned((up_two, down_two, ends))

    far = [across(part, 3, 0, (0, 3)) for part in ends]
    second = jnp.where(lax.axis_index("img") < 2 * PLANE, down_two, up_two)
    packing = [
        (own_image, other(2, 0), other(0, change), slot, always, change - 1, slot)
        for change in changes
        for slot in slots
    ]
    packed = pack_for(packing, (second,), PLANE - 1)
    packed, near = pinned((packed, near))
    third = to_others(packed)
    branches = [
        (
            hopped(1, 0) if change == 0 else fixed(1 + change, slot),
            other(1, change),
            slot,
            always,
        )
        for change in range(PLANE)
        for slot in slots
    ] + [
        (
            hopped(3, 0) if change == 0 else fixed(PLANE + change, slot),
            other(3, change),
            slot,
            inner,
        )
        for change in range(PLANE)
        for slot in slots
    ]
    sums = run_branches(
        branches, tables, devices, length, (up_one, down_one, *near, *cross), shared, sums
    )
    branches = [
        (own_image if change == 0 else fixed(change, slot), other(2, change), slot, always)
        for change in range(PLANE)
        for slot in slots
    ]
    sums = run_branches(branches, tables, devices, length, (second, *third), shared, sums)
    branches = [
        (fixed(change // 2, change % 2 * SLOTS + slot), other(3, change), slot, outer)
        for change in range(PLANE)
        for slot in slots
    ]
    return run_branches(branches, tables, devices, length, tuple(far), shared, sums, tokens)


def local(
    tokens, pair_list, w_query, w_key, w_value, w_out, gain_query, context_norm_gain, conf_weight
):
    per_device, length, feats = tokens.shape
    devices = lax.axis_size("img")
    me = lax.axis_index("img")
    firsts, seconds = pair_tables(pair_list, per_device, devices)
    tables = (firsts.reshape(-1), seconds.reshape(-1), me.astype(jnp.int32)[None])

    def shared_of():
        q_t, tok_conf = prepare(tokens, w_query.T, gain_query, conf_weight)
        return (
            tok_conf,
            context_norm_gain[None, :],
            jnp.broadcast_to(conf_weight[:, None], (feats, 128)),
            q_t,
            w_key,
            w_value.T,
            w_out.T,
        )

    if devices == 4 * PLANE:
        merged = line_exchange(tokens, tables, devices, shared_of)
    else:
        merged = dense_exchange(tokens, tables, devices, shared_of())
    merged = merged.reshape(length, feats // 128, per_device, 128)
    return jnp.transpose(merged, (2, 0, 1, 3)).reshape(per_device, length, feats)


def solution(mesh):
    return jax.shard_map(
        local,
        mesh=mesh,
        in_specs=(P(("groups", "img"), None, None), P(("groups", "img"), None)) + (P(),) * 7,
        out_specs=P(("groups", "img"), None, None),
        check_vma=False,
    )
```

profile of v0, /device:TPU:7, one launch (start us, length us, event | category | flops | bytes accessed | tf_op | source)
XLA Modules:
  0.0 247.2 jit_solution(1452684481135935113)
XLA Ops:
  0.0 18.6 %all-gather.1 = s32[16,8,2]{1,2,0:T(2,128)S(1)} all-gather(s32[1,8,2]{1,2,0:T(2,128)} %bitcast.25), channel_id=2, replica_groups=mesh['groups'=2,'img'=16] {'img'}, dimensions={0}, use_global_device_ids=true | all-gather | bytes 1088 | tf_op jit(solution)/shard_map/all_gather | solution.py:411
  24.5 3.6 %copy.52.refs_0_.refs_11_ = bf16[8,196,768]{2,1,0:T(8,128)(2,1)} copy(bf16[8,196,768]{2,0,1:T(8,128)(2,1)} %param.9) | data formatting | bytes 4816896 | tf_op jit(solution)/shard_map/optimization_barrier | solution.py:499
  28.1 3.1 %pack_images.4 = (bf16[400,768]{1,0:T(8,128)(2,1)}, bf16[400,768]{1,0:T(8,128)(2,1)}, bf16[400,768]{1,0:T(8,128)(2,1)}) custom-call(s32[256]{0:T(256)} %reshape.26.firsts_ref, s32[256]{0:T(256)} %reshape.27.seconds_ref, s32[1]{0:T(128)} %bitcast.4.me_ref, bf16[8,196,768]{2,1,0:T(8,128)(2,1)} %copy.52.refs_0_.refs_11_), custom_call_target="tpu_custom_call" | custom-call | tf_op jit(solution)/shard_map/pack_images/pallas_call | solution.py:322
  31.8 3.4 %collective-permute-start.3 = (bf16[400,768]{1,0:T(8,128)(2,1)}, bf16[400,768]{1,0:T(8,128)(2,1)}, u32[]{:S(2)}, u32[]{:S(2)}) collective-permute-start(bf16[400,768]{1,0:T(8,128)(2,1)} %get-tuple-element.76), channel_id=1, source_target_pairs={{0,2},{1,3},{2,0},{3,1},{4,6},{5,7},{6,4},{7,5},{8,10},{9,11},{10,... | collective-permute-start | bytes 1843208 | tf_op jit(solution)/shard_map/ppermute | solution.py:464
  43.7 9.5 %own_queries.1 = (bf16[8,768,256]{2,1,0:T(8,128)(2,1)}, f32[8,1,256]{2,1,0:T(1,128)}) custom-call(bf16[8,196,768]{2,1,0:T(8,128)(2,1)} %copy.54.tokens_ref, bf16[768,768]{1,0:T(8,128)(2,1)} %bitcast.24, f32[1,768]{1,0:T(1,128)} %broadcast_in_dim.51.gain_ref, f32[1,768]{1,0:T(1,128)} %broadcast_in_dim.52.conf_row_ref), custom_call_target="tpu_custom_call" | custom-call | tf_op jit(solution)/shard_map/own_queries/pallas_call | solution.py:396
  53.3 9.9 %collective-permute-done.4.refs_3_ = bf16[400,768]{1,0:T(8,128)(2,1)} collective-permute-done((bf16[400,768]{1,0:T(8,128)(2,1)}, bf16[400,768]{1,0:T(8,128)(2,1)}, u32[]{:S(2)}, u32[]{:S(2)}) %collective-permute-start.4) | collective-permute-done | bytes 614432 | tf_op jit(solution)/shard_map/ppermute | solution.py:464
  63.2 10.7 %collective-permute-done = bf16[8,196,768]{2,0,1:T(8,128)(2,1)} collective-permute-done((bf16[8,196,768]{2,0,1:T(8,128)(2,1)}, bf16[8,196,768]{2,0,1:T(8,128)(2,1)}, u32[]{:S(2)}, u32[]{:S(2)}) %collective-permute-start) | collective-permute-done | bytes 2408480 | tf_op jit(solution)/shard_map/ppermute | solution.py:457
  73.9 5.3 %collective-permute-done.1 = bf16[8,196,768]{2,0,1:T(8,128)(2,1)} collective-permute-done((bf16[8,196,768]{2,0,1:T(8,128)(2,1)}, bf16[8,196,768]{2,0,1:T(8,128)(2,1)}, u32[]{:S(2)}, u32[]{:S(2)}) %collective-permute-start.1) | collective-permute-done | bytes 2408480 | tf_op jit(solution)/shard_map/ppermute | solution.py:457
  82.2 3.6 %copy.58.refs_1_.refs_0_ = bf16[8,196,768]{2,1,0:T(8,128)(2,1)} copy(bf16[8,196,768]{2,0,1:T(8,128)(2,1)} %collective-permute-done) | data formatting | bytes 4816896 | tf_op jit(solution)/shard_map/optimization_barrier | solution.py:509
  85.8 3.6 %copy.59.refs_2_.refs_1_ = bf16[8,196,768]{2,1,0:T(8,128)(2,1)} copy(bf16[8,196,768]{2,0,1:T(8,128)(2,1)} %collective-permute-done.1) | data formatting | bytes 4816896 | tf_op jit(solution)/shard_map/optimization_barrier | solution.py:509
  89.3 3.7 %pack_images.5 = (bf16[400,768]{1,0:T(8,128)(2,1)}, bf16[400,768]{1,0:T(8,128)(2,1)}, bf16[400,768]{1,0:T(8,128)(2,1)}, bf16[400,768]{1,0:T(8,128)(2,1)}, bf16[4...) custom-call(s32[256]{0:T(256)} %reshape.26.firsts_ref, s32[256]{0:T(256)} %reshape.27.seconds_ref, s32[1]{0:T(128)} %bitcast.4.me_ref, ...), custom_call_target="tpu_custom_call" | custom-call | tf_op jit(solution)/shard_map/pack_images/pallas_call | solution.py:322
  93.7 3.9 %collective-permute-start.8 = (bf16[400,768]{1,0:T(8,128)(2,1)}, bf16[400,768]{1,0:T(8,128)(2,1)}, u32[]{:S(2)}, u32[]{:S(2)}) collective-permute-start(bf16[400,768]{1,0:T(8,128)(2,1)} %get-tuple-element.90), channel_id=1, source_target_pairs={{0,2},{1,3},{2,0},{3,1},{4,6},{5,7},{6,4},{7,5},{8,10},{9,11},{10,... | collective-permute-start | bytes 1843208 | tf_op jit(solution)/shard_map/ppermute | solution.py:464
  97.7 23.7 %attend_branches.4 = (f32[8,768,256]{2,1,0:T(8,128)}, f32[8,1,256]{2,1,0:T(1,128)}) custom-call(s32[256]{0:T(256)} %reshape.26.firsts_ref, s32[256]{0:T(256)} %reshape.27.seconds_ref, s32[1]{0:T(128)} %bitcast.4.me_ref, bf16[8,196,768]{2,1,0:T(8,128)(2,1)} %copy.52.refs_0_.refs_11_, bf16[400,768]{1,0:T(8,128)(2,1)} %collective-permute-done.2.refs_1_, ...), custom_call_target="tpu_custom_call" | custom-call | flops 5200000000 | bytes 8000000 | tf_op jit(solution)/shard_map/attend_branches/pallas_call | solution.py:377
  121.4 4.1 %collective-permute-done.9.refs_3_.refs_7_ = bf16[400,768]{1,0:T(8,128)(2,1)} collective-permute-done((bf16[400,768]{1,0:T(8,128)(2,1)}, bf16[400,768]{1,0:T(8,128)(2,1)}, u32[]{:S(2)}, u32[]{:S(2)}) %collective-permute-start.9) | collective-permute-done | bytes 614432 | tf_op jit(solution)/shard_map/ppermute | solution.py:464
  125.5 5.9 %collective-permute-start.12 = (bf16[400,768]{1,0:T(8,128)(2,1)}, bf16[400,768]{1,0:T(8,128)(2,1)}, u32[]{:S(2)}, u32[]{:S(2)}) collective-permute-start(bf16[400,768]{1,0:T(8,128)(2,1)} %get-tuple-element.122), channel_id=1, source_target_pairs={{0,1},{1,0},{2,3},{3,2},{4,5},{5,4},{6,7},{7,6},{8,9},{9,8},{10,11... | collective-permute-start | bytes 1843208 | tf_op jit(solution)/shard_map/ppermute | solution.py:464
  133.1 3.0 %pack_images.6 = (bf16[800,768]{1,0:T(8,128)(2,1)}, bf16[800,768]{1,0:T(8,128)(2,1)}) custom-call(s32[256]{0:T(256)} %reshape.26.firsts_ref, s32[256]{0:T(256)} %reshape.27.seconds_ref, s32[1]{0:T(128)} %bitcast.4.me_ref, bf16[8,196,768]{2,1,0:T(8,128)(2,1)} %copy.52.refs_0_.refs_11_, bf16[400,768]{1,0:T(8,128)(2,1)} %copy-done.6, ...), custom_call_target="tpu_custom_call" | custom-call | tf_op jit(solution)/shard_map/pack_images/pallas_call | solution.py:322
  138.2 5.3 %collective-permute-start.11 = (bf16[800,768]{1,0:T(8,128)(2,1)}, bf16[800,768]{1,0:T(8,128)(2,1)S(1)}, u32[]{:S(2)}, u32[]{:S(2)}) collective-permute-start(bf16[800,768]{1,0:T(8,128)(2,1)} %get-tuple-element.116), channel_id=1, source_target_pairs={{0,12},{1,13},{2,14},{3,15},{12,0},{13,1},{14,2},{15,3},{16,28},{1... | collective-permute-start | bytes 3686408 | tf_op jit(solution)/shard_map/ppermute | solution.py:464
  143.5 4.6 %copy_select_fusion.refs_0_ = bf16[8,196,768]{2,1,0:T(8,128)(2,1)} fusion(bf16[8,196,768]{2,0,1:T(8,128)(2,1)S(1)} %collective-permute-done.5, bf16[8,196,768]{2,0,1:T(8,128)(2,1)} %collective-permute-done.6, pred[]{:T(512)S(6)} %lt.3), kind=kLoop, calls=%fused_computation | loop fusion | flops 1204224 | bytes 7225345 | tf_op jit(solution)/shard_map/jit(_where)/select_n | solution.py:551
  150.9 9.8 %collective-permute-done.14.refs_4_ = bf16[400,768]{1,0:T(8,128)(2,1)} collective-permute-done((bf16[400,768]{1,0:T(8,128)(2,1)}, bf16[400,768]{1,0:T(8,128)(2,1)}, u32[]{:S(2)}, u32[]{:S(2)}) %collective-permute-start.14) | collective-permute-done | bytes 614432 | tf_op jit(solution)/shard_map/ppermute | solution.py:464
  162.8 8.9 %attend_branches.5 = (f32[8,768,256]{2,1,0:T(8,128)}, f32[8,1,256]{2,1,0:T(1,128)}) custom-call(s32[256]{0:T(256)} %reshape.26.firsts_ref, s32[256]{0:T(256)} %reshape.27.seconds_ref, s32[1]{0:T(128)} %bitcast.4.me_ref, bf16[8,196,768]{2,1,0:T(8,128)(2,1)} %copy.58.refs_1_.refs_0_, bf16[8,196,768]{2,1,0:T(8,128)(2,1)} %copy.59.refs_2_.refs_1_, ...), custom_call_target="tpu_custom_call" | custom-call | flops 10400000000 | bytes 16000000 | tf_op jit(solution)/shard_map/attend_branches/pallas_call | solution.py:377
  171.7 4.2 %collective-permute-done.16.refs_2_ = bf16[400,768]{1,0:T(8,128)(2,1)S(1)} collective-permute-done((bf16[400,768]{1,0:T(8,128)(2,1)}, bf16[400,768]{1,0:T(8,128)(2,1)S(1)}, u32[]{:S(2)}, u32[]{:S(2)}) %collective-permute-start.16) | collective-permute-done | bytes 614432 | tf_op jit(solution)/shard_map/ppermute | solution.py:464
  175.9 14.1 %collective-permute-done.17.refs_3_ = bf16[400,768]{1,0:T(8,128)(2,1)S(1)} collective-permute-done((bf16[400,768]{1,0:T(8,128)(2,1)}, bf16[400,768]{1,0:T(8,128)(2,1)S(1)}, u32[]{:S(2)}, u32[]{:S(2)}) %collective-permute-start.17) | collective-permute-done | bytes 614432 | tf_op jit(solution)/shard_map/ppermute | solution.py:464
  190.8 20.0 %attend_branches.6 = (f32[8,768,256]{2,1,0:T(8,128)}, f32[8,1,256]{2,1,0:T(1,128)}) custom-call(s32[256]{0:T(256)} %reshape.26.firsts_ref, s32[256]{0:T(256)} %reshape.27.seconds_ref, s32[1]{0:T(128)} %bitcast.4.me_ref, bf16[8,196,768]{2,1,0:T(8,128)(2,1)} %copy_select_fusion.refs_0_, bf16[400,768]{1,0:T(8,128)(2,1)} %copy-done.10, ...), custom_call_target="tpu_custom_call" | custom-call | flops 5200000000 | bytes 8000000 | tf_op jit(solution)/shard_map/attend_branches/pallas_call | solution.py:377
  212.3 34.7 %attend_branches.7 = f32[9408,128]{1,0:T(8,128)} custom-call(s32[256]{0:T(256)} %reshape.26.firsts_ref, s32[256]{0:T(256)} %reshape.27.seconds_ref, s32[1]{0:T(128)} %bitcast.4.me_ref, bf16[800,768]{1,0:T(8,128)(2,1)} %copy-done.1, bf16[800,768]{1,0:T(8,128)(2,1)} %copy-done.2, f32[8,1,256]{2,1,0:T(1,128)} %get-tuple-element.101.refs_4_.refs_8_.refs_2_, ...), custom_call_target="tpu_custom_call" | custom-call | flops 5200000000 | bytes 8000000 | tf_op jit(solution)/shard_map/attend_branches/pallas_call | solution.py:377
  (72 shorter events, 29.7 us)
Async XLA Ops:
  20.5 53.4 %collective-permute-start = (bf16[8,196,768]{2,0,1:T(8,128)(2,1)}, bf16[8,196,768]{2,0,1:T(8,128)(2,1)}, u32[]{:S(2)}, u32[]{:S(2)}) collective-permute-start(bf16[8,196,768]{2,0,1:T(8,128)(2,1)} %param.9), channel_id=1, source_target_pairs={{0,4},{1,5},{2,6},{3,7},{4,8},{5,9},{6,10},{7,11},{8,12},{9,13},{1... | collective-permute-start | bytes 7225352 | tf_op jit(solution)/shard_map/ppermute | solution.py:457
  23.3 55.9 %collective-permute-start.1 = (bf16[8,196,768]{2,0,1:T(8,128)(2,1)}, bf16[8,196,768]{2,0,1:T(8,128)(2,1)}, u32[]{:S(2)}, u32[]{:S(2)}) collective-permute-start(bf16[8,196,768]{2,0,1:T(8,128)(2,1)} %param.9), channel_id=1, source_target_pairs={{4,0},{5,1},{6,2},{7,3},{8,4},{9,5},{10,6},{11,7},{12,8},{13,9},{1... | collective-permute-start | bytes 7225352 | tf_op jit(solution)/shard_map/ppermute | solution.py:457
  28.1 7.6 %copy-start = (bf16[8,196,768]{2,0,1:T(8,128)(2,1)S(1)}, bf16[8,196,768]{2,0,1:T(8,128)(2,1)}, u32[]{:S(2)}) copy-start(bf16[8,196,768]{2,0,1:T(8,128)(2,1)} %param.9) | copy-start | bytes 7225348
  31.2 22.1 %collective-permute-start.2 = (bf16[400,768]{1,0:T(8,128)(2,1)}, bf16[400,768]{1,0:T(8,128)(2,1)}, u32[]{:S(2)}, u32[]{:S(2)}) collective-permute-start(bf16[400,768]{1,0:T(8,128)(2,1)} %get-tuple-element.75), channel_id=1, source_target_pairs={{0,1},{1,0},{2,3},{3,2},{4,5},{5,4},{6,7},{7,6},{8,9},{9,8},{10,11... | collective-permute-start | bytes 1843208 | tf_op jit(solution)/shard_map/ppermute | solution.py:464
  31.8 21.4 %collective-permute-start.3 = (bf16[400,768]{1,0:T(8,128)(2,1)}, bf16[400,768]{1,0:T(8,128)(2,1)}, u32[]{:S(2)}, u32[]{:S(2)}) collective-permute-start(bf16[400,768]{1,0:T(8,128)(2,1)} %get-tuple-element.76), channel_id=1, source_target_pairs={{0,2},{1,3},{2,0},{3,1},{4,6},{5,7},{6,4},{7,5},{8,10},{9,11},{10,... | collective-permute-start | bytes 1843208 | tf_op jit(solution)/shard_map/ppermute | solution.py:464
  35.3 5.0 %copy-start.9 = (f32[768]{0:T(1024)S(1)}, f32[768]{0:T(1024)}, u32[]{:S(2)}) copy-start(f32[768]{0:T(1024)} %param.16) | copy-start | bytes 9220
  35.3 5.6 %copy-start.4 = (bf16[768,768]{1,0:T(8,128)(2,1)S(1)}, bf16[768,768]{1,0:T(8,128)(2,1)}, u32[]{:S(2)}) copy-start(bf16[768,768]{1,0:T(8,128)(2,1)} %param.13) | copy-start | bytes 3538948
  35.3 27.9 %collective-permute-start.4 = (bf16[400,768]{1,0:T(8,128)(2,1)}, bf16[400,768]{1,0:T(8,128)(2,1)}, u32[]{:S(2)}, u32[]{:S(2)}) collective-permute-start(bf16[400,768]{1,0:T(8,128)(2,1)} %get-tuple-element.77), channel_id=1, source_target_pairs={{0,3},{1,2},{2,1},{3,0},{4,7},{5,6},{6,5},{7,4},{8,11},{9,10},{10,... | collective-permute-start | bytes 1843208 | tf_op jit(solution)/shard_map/ppermute | solution.py:464
  80.1 56.0 %collective-permute-start.5 = (bf16[8,196,768]{2,0,1:T(8,128)(2,1)}, bf16[8,196,768]{2,0,1:T(8,128)(2,1)S(1)}, u32[]{:S(2)}, u32[]{:S(2)}) collective-permute-start(bf16[8,196,768]{2,0,1:T(8,128)(2,1)} %collective-permute-done), channel_id=1, source_target_pairs={{4,8},{5,9},{6,10},{7,11},{8,12},{9,13},{10,14},{11,15},{20,24},{2... | collective-permute-start | bytes 7225352 | tf_op jit(solution)/shard_map/ppermute | solution.py:457
  80.9 55.4 %collective-permute-start.6 = (bf16[8,196,768]{2,0,1:T(8,128)(2,1)}, bf16[8,196,768]{2,0,1:T(8,128)(2,1)}, u32[]{:S(2)}, u32[]{:S(2)}) collective-permute-start(bf16[8,196,768]{2,0,1:T(8,128)(2,1)} %collective-permute-done.1), channel_id=1, source_target_pairs={{4,0},{5,1},{6,2},{7,3},{8,4},{9,5},{10,6},{11,7},{20,16},{21,17},... | collective-permute-start | bytes 7225352 | tf_op jit(solution)/shard_map/ppermute | solution.py:457
  93.0 28.3 %collective-permute-start.7 = (bf16[400,768]{1,0:T(8,128)(2,1)}, bf16[400,768]{1,0:T(8,128)(2,1)S(1)}, u32[]{:S(2)}, u32[]{:S(2)}) collective-permute-start(bf16[400,768]{1,0:T(8,128)(2,1)} %get-tuple-element.89), channel_id=1, source_target_pairs={{0,1},{1,0},{2,3},{3,2},{4,5},{5,4},{6,7},{7,6},{8,9},{9,8},{10,11... | collective-permute-start | bytes 1843208 | tf_op jit(solution)/shard_map/ppermute | solution.py:464
  93.7 27.7 %collective-permute-start.8 = (bf16[400,768]{1,0:T(8,128)(2,1)}, bf16[400,768]{1,0:T(8,128)(2,1)}, u32[]{:S(2)}, u32[]{:S(2)}) collective-permute-start(bf16[400,768]{1,0:T(8,128)(2,1)} %get-tuple-element.90), channel_id=1, source_target_pairs={{0,2},{1,3},{2,0},{3,1},{4,6},{5,7},{6,4},{7,5},{8,10},{9,11},{10,... | collective-permute-start | bytes 1843208 | tf_op jit(solution)/shard_map/ppermute | solution.py:464
  97.6 27.9 %collective-permute-start.9 = (bf16[400,768]{1,0:T(8,128)(2,1)}, bf16[400,768]{1,0:T(8,128)(2,1)}, u32[]{:S(2)}, u32[]{:S(2)}) collective-permute-start(bf16[400,768]{1,0:T(8,128)(2,1)} %get-tuple-element.91), channel_id=1, source_target_pairs={{0,3},{1,2},{2,1},{3,0},{4,7},{5,6},{6,5},{7,4},{8,11},{9,10},{10,... | collective-permute-start | bytes 1843208 | tf_op jit(solution)/shard_map/ppermute | solution.py:464
  121.4 11.7 %copy-start.6 = (bf16[400,768]{1,0:T(8,128)(2,1)}, bf16[400,768]{1,0:T(8,128)(2,1)S(1)}, u32[]{:S(2)}) copy-start(bf16[400,768]{1,0:T(8,128)(2,1)S(1)} %collective-permute-done.7.refs_1_.refs_5_) | copy-start | bytes 1843204
  125.5 25.4 %collective-permute-start.12 = (bf16[400,768]{1,0:T(8,128)(2,1)}, bf16[400,768]{1,0:T(8,128)(2,1)}, u32[]{:S(2)}, u32[]{:S(2)}) collective-permute-start(bf16[400,768]{1,0:T(8,128)(2,1)} %get-tuple-element.122), channel_id=1, source_target_pairs={{0,1},{1,0},{2,3},{3,2},{4,5},{5,4},{6,7},{7,6},{8,9},{9,8},{10,11... | collective-permute-start | bytes 1843208 | tf_op jit(solution)/shard_map/ppermute | solution.py:464
  131.4 19.4 %collective-permute-start.13 = (bf16[400,768]{1,0:T(8,128)(2,1)}, bf16[400,768]{1,0:T(8,128)(2,1)}, u32[]{:S(2)}, u32[]{:S(2)}) collective-permute-start(bf16[400,768]{1,0:T(8,128)(2,1)} %get-tuple-element.123), channel_id=1, source_target_pairs={{0,2},{1,3},{2,0},{3,1},{4,6},{5,7},{6,4},{7,5},{8,10},{9,11},{10,... | collective-permute-start | bytes 1843208 | tf_op jit(solution)/shard_map/ppermute | solution.py:464
  131.4 29.3 %collective-permute-start.14 = (bf16[400,768]{1,0:T(8,128)(2,1)}, bf16[400,768]{1,0:T(8,128)(2,1)}, u32[]{:S(2)}, u32[]{:S(2)}) collective-permute-start(bf16[400,768]{1,0:T(8,128)(2,1)} %get-tuple-element.124), channel_id=1, source_target_pairs={{0,3},{1,2},{2,1},{3,0},{4,7},{5,6},{6,5},{7,4},{8,11},{9,10},{10,... | collective-permute-start | bytes 1843208 | tf_op jit(solution)/shard_map/ppermute | solution.py:464
  136.3 74.6 %collective-permute-start.10 = (bf16[800,768]{1,0:T(8,128)(2,1)}, bf16[800,768]{1,0:T(8,128)(2,1)S(1)}, u32[]{:S(2)}, u32[]{:S(2)}) collective-permute-start(bf16[800,768]{1,0:T(8,128)(2,1)} %get-tuple-element.115), channel_id=1, source_target_pairs={{0,12},{1,13},{2,14},{3,15},{12,0},{13,1},{14,2},{15,3},{16,28},{1... | collective-permute-start | bytes 3686408 | tf_op jit(solution)/shard_map/ppermute | solution.py:464
  138.2 72.7 %collective-permute-start.11 = (bf16[800,768]{1,0:T(8,128)(2,1)}, bf16[800,768]{1,0:T(8,128)(2,1)S(1)}, u32[]{:S(2)}, u32[]{:S(2)}) collective-permute-start(bf16[800,768]{1,0:T(8,128)(2,1)} %get-tuple-element.116), channel_id=1, source_target_pairs={{0,12},{1,13},{2,14},{3,15},{12,0},{13,1},{14,2},{15,3},{16,28},{1... | collective-permute-start | bytes 3686408 | tf_op jit(solution)/shard_map/ppermute | solution.py:464
  160.7 11.0 %collective-permute-start.15 = (bf16[400,768]{1,0:T(8,128)(2,1)}, bf16[400,768]{1,0:T(8,128)(2,1)S(1)}, u32[]{:S(2)}, u32[]{:S(2)}) collective-permute-start(bf16[400,768]{1,0:T(8,128)(2,1)} %get-tuple-element.125), channel_id=1, source_target_pairs={{0,1},{1,0},{2,3},{3,2},{4,5},{5,4},{6,7},{7,6},{8,9},{9,8},{10,11... | collective-permute-start | bytes 1843208 | tf_op jit(solution)/shard_map/ppermute | solution.py:464
  160.7 15.2 %collective-permute-start.16 = (bf16[400,768]{1,0:T(8,128)(2,1)}, bf16[400,768]{1,0:T(8,128)(2,1)S(1)}, u32[]{:S(2)}, u32[]{:S(2)}) collective-permute-start(bf16[400,768]{1,0:T(8,128)(2,1)} %get-tuple-element.126), channel_id=1, source_target_pairs={{0,2},{1,3},{2,0},{3,1},{4,6},{5,7},{6,4},{7,5},{8,10},{9,11},{10,... | collective-permute-start | bytes 1843208 | tf_op jit(solution)/shard_map/ppermute | solution.py:464
  160.9 29.1 %collective-permute-start.17 = (bf16[400,768]{1,0:T(8,128)(2,1)}, bf16[400,768]{1,0:T(8,128)(2,1)S(1)}, u32[]{:S(2)}, u32[]{:S(2)}) collective-permute-start(bf16[400,768]{1,0:T(8,128)(2,1)} %get-tuple-element.127), channel_id=1, source_target_pairs={{0,3},{1,2},{2,1},{3,0},{4,7},{5,6},{6,5},{7,4},{8,11},{9,10},{10,... | collective-permute-start | bytes 1843208 | tf_op jit(solution)/shard_map/ppermute | solution.py:464
  171.7 18.3 %copy-start.10 = (bf16[400,768]{1,0:T(8,128)(2,1)}, bf16[400,768]{1,0:T(8,128)(2,1)S(1)}, u32[]{:S(2)}) copy-start(bf16[400,768]{1,0:T(8,128)(2,1)S(1)} %collective-permute-done.15.refs_1_) | copy-start | bytes 1843204
  175.9 14.1 %copy-start.11 = (bf16[400,768]{1,0:T(8,128)(2,1)}, bf16[400,768]{1,0:T(8,128)(2,1)S(1)}, u32[]{:S(2)}) copy-start(bf16[400,768]{1,0:T(8,128)(2,1)S(1)} %collective-permute-done.16.refs_2_) | copy-start | bytes 1843204
  (7 other events, 18.5 us)
where the time goes:
time: 248 us; the launch traced here: 247 us
  Pallas kernels  109 us (44%)
  waiting for transfers between devices  58.2 us (23%)
  starting transfers between devices  32.2 us (13%)
  local copies, waits for them, and re-layouts  23.7 us (10%)
  blocking collectives  18.6 us (8%)
  other arithmetic  4.72 us (2%)
    pallas_call x4, Pallas kernels, run_branches(): pl.pallas_call(functools.partial(branch_kernel, plan, devices, len(partne...  87.3 us
    ppermute x14, waiting for transfers between devices, across(): lax.ppermute(array, 'img', [(p * PLANE + c, (p ^ flip) * PLANE + (c ^ cha...  42 us
    ppermute x14, starting transfers between devices, across(): lax.ppermute(array, 'img', [(p * PLANE + c, (p ^ flip) * PLANE + (c ^ cha...  26.1 us
    all_gather x1, blocking collectives, pair_tables(): pairs = lax.all_gather(pair_list, 'img', axis=0, tiled=False)  18.6 us
    ppermute x4, waiting for transfers between devices, hop(): lax.ppermute(array, 'img', [(p * PLANE + c, (p + step) * PLANE + c) for p...  16.1 us
    pallas_call x4, Pallas kernels, pack(): pl.pallas_call(functools.partial(pack_kernel, plan, devices, len(sources)...  12.5 us
    pallas_call x1, Pallas kernels, prepare(): pl.pallas_call(prep_kernel, out_shape=(jax.ShapeDtypeStruct((images, feat...  9.54 us
    unnamed x32, local copies, waits for them, and re-layouts  8.7 us
  transfers between devices with their start and end apart: 18, of which 8 were waited for; matrix products, arithmetic and copies ran while one was open for 9% of the time, Pallas kernels for 30%

commit v1 on v0

--- a/solution.py
+++ b/solution.py
@@ -84,34 +84,36 @@
     partner_refs = refs[:sources]
     rest = list(refs[sources:])
     tok_conf_ref, gain_ref, conf_col_ref = rest[:3]
-    stored = rest[3:7]
+    q_t_in = rest[3]
+    stored = rest[4:7]
     rest = rest[7:]
     if not first_call:
         denom_in, numer_in = rest[:2]
         rest = rest[2:]
     if last_call:
         tokens_in, merged_ref = rest[:2]
-        numer, denom, tokens_ref = rest[2:5]
-        rest = rest[5:]
+        numer, denom, tokens_ref, earlier = rest[2:6]
+        rest = rest[6:]
     else:
         numer, denom = rest[:2]
         rest = rest[2:]
-    q_t_ref, wk_ref, wv_t_ref, wo_t_ref = loaded = rest[:4]
+    q_t_ref, wk_ref, wv_t_ref, wo_t_ref = rest[:4]
     listed, whole_arrived, arrived, normed, keys, values_t, scores, probs, mixed_t = rest[4:13]
-    copy_sem, load_sem = rest[13:]
+    copy_sem, query_sem, load_sem = rest[13:]
     loads = [
         pltpu.make_async_copy(origin, target, load_sem.at[turn])
-        for turn, (origin, target) in enumerate(zip(stored, loaded))
-    ]
-    if not first_call:
-        loads.append(pltpu.make_async_copy(numer_in, numer, load_sem.at[4]))
-    for turn in (1, 2, 0, 3, 4):
-        if turn < len(loads):
-            loads[turn].start()
+        for turn, (origin, target) in enumerate(zip(stored, rest[1:4]))
+    ]
+    late_loads = []
+    if not first_call and not last_call:
+        loads.append(pltpu.make_async_copy(numer_in, numer, load_sem.at[3]))
+    if not first_call and last_call:
+        late_loads.append(pltpu.make_async_copy(numer_in, earlier, load_sem.at[3]))
     if last_call:
-        tokens_load = pltpu.make_async_copy(tokens_in, tokens_ref, load_sem.at[5])
-        tokens_load.start()
-    images, feats, lanes = q_t_ref.shape
+        late_loads.append(pltpu.make_async_copy(tokens_in, tokens_ref, load_sem.at[4]))
+    for load in loads + late_loads:
+        load.start()
+    images, feats, lanes = numer.shape
     length, rows = whole_arrived.shape[1], arrived.shape[1]
     key_rows = keys.shape[0]
     head_dim = feats // HEADS
@@ -154,8 +156,15 @@
     def finish(copy):
         copy.wait()
 
+    def queries_of(turn):
+        slot = turn % 2
+        return pltpu.make_async_copy(
+            q_t_in.at[listed[turn, 2]], q_t_ref.at[slot], query_sem.at[slot]
+        )
+
     def fetch(turn):
         copies(turn, begin)
+        queries_of(turn).start()
 
     @pl.when(total > 0)
     def _():
@@ -163,11 +172,9 @@
 
     normed[...] = jnp.zeros_like(normed)
     probs[:, key_rows:, :] = jnp.zeros((HEADS, lanes - key_rows, lanes), jnp.bfloat16)
-    if first_call:
+    if first_call or last_call:
         numer[...] = jnp.zeros_like(numer)
-        denom[...] = jnp.ones_like(denom)
-    else:
-        denom[...] = denom_in[...]
+    denom[...] = jnp.ones_like(denom) if first_call else denom_in[...]
 
     tail_rows = lax.broadcasted_iota(jnp.int32, (key_rows - whole, 128), 0) + whole
     tail_ok = tail_rows < length
@@ -175,24 +182,17 @@
     def one_branch(turn, carry):
         slot = turn % 2
         copies(turn, finish)
+        queries_of(turn).wait()
 
         @pl.when(turn + 1 < total)
         def _():
             fetch(turn + 1)
 
         image = listed[turn, 2]
-
-        def loaded_by_now(which):
-            @pl.when(turn == 0)
-            def _():
-                loads[which].wait()
-
         normed[0:length, :] = (centred_scaled(arrived[slot, 0:length, :]) * gain_ref[...]).astype(jnp.bfloat16)
-        loaded_by_now(1)
         keys[...] = jnp.dot(
             normed[0:key_rows, :], wk_ref[...], preferred_element_type=jnp.float32
         ).astype(jnp.bfloat16)
-        loaded_by_now(2)
         values_t[...] = lax.dot_general(
             wv_t_ref[...],
             normed[...],
@@ -200,9 +200,8 @@
             preferred_element_type=jnp.float32,
         ).astype(jnp.bfloat16)
         zero_rows = jnp.zeros((head_dim, lanes), jnp.bfloat16)
-        loaded_by_now(0)
         for head in range(HEADS):
-            own_q = q_t_ref[image, head * head_dim : (head + 1) * head_dim, :]
+            own_q = q_t_ref[slot, head * head_dim : (head + 1) * head_dim, :]
             pair = head // 2
             ordered = [own_q, zero_rows] if head % 2 == 0 else [zero_rows, own_q]
             scores[head] = jnp.dot(
@@ -233,7 +232,6 @@
             mixed_t[part, :] = jnp.dot(
                 values_t[part, :], probs[head], preferred_element_type=jnp.float32
             ).astype(jnp.bfloat16)
-        loaded_by_now(3)
         update = (
             jnp.dot(wo_t_ref[...], mixed_t[...], preferred_element_type=jnp.float32)
             .astype(jnp.bfloat16)
@@ -247,23 +245,20 @@
             axis=1,
         )
         conf = 1.0 + jnp.maximum(logit, 0.0) + jnp.log1p(jnp.exp(-jnp.abs(logit)))
-        if not first_call:
-            loaded_by_now(4)
         numer[image] += conf * update
         denom[image] += conf
         return carry
 
+    for load in loads:
+        load.wait()
     lax.fori_loop(0, total, one_branch, 0)
 
-    @pl.when(total == 0)
-    def _():
-        for load in loads:
+    if last_call:
+        for load in late_loads:
             load.wait()
-
-    if last_call:
-        tokens_load.wait()
         for image in range(images):
-            ratio = jnp.transpose(numer[image] * (1.0 / denom[image]))
+            total_numer = numer[image] if first_call else numer[image] + earlier[image]
+            ratio = jnp.transpose(total_numer * (1.0 / denom[image]))
             merged = tokens_ref[image].astype(jnp.float32) + ratio[0:length, :]
             for part in range(feats // 128):
                 merged_ref[
@@ -356,10 +351,12 @@
         outs = jax.ShapeDtypeStruct((length * images * feats // 128, 128), jnp.float32)
         out_specs = VMEM
         scratch = [pltpu.VMEM(k.shape, k.dtype) for k in (*kept, tokens)]
+        scratch.append(pltpu.VMEM(kept[0].shape if sums is not None else (8, 128), jnp.float32))
     else:
         outs, out_specs = kept, (VMEM, VMEM)
     key_rows = round_up(length, 16)
-    scratch += [pltpu.VMEM(k.shape, k.dtype) for k in shared[3:]]
+    scratch.append(pltpu.VMEM((2, feats, lanes), jnp.bfloat16))
+    scratch += [pltpu.VMEM(k.shape, k.dtype) for k in shared[4:]]
     scratch += [
         pltpu.SMEM((len(plan), 3), jnp.int32),
         pltpu.VMEM((2, length, feats), jnp.bfloat16),
@@ -371,7 +368,8 @@
         pltpu.VMEM((HEADS, lanes, lanes), jnp.bfloat16),
         pltpu.VMEM((feats, lanes), jnp.bfloat16),
         pltpu.SemaphoreType.DMA((2,)),
-        pltpu.SemaphoreType.DMA((6,)),
+        pltpu.SemaphoreType.DMA((2,)),
+        pltpu.SemaphoreType.DMA((5,)),
     ]
     expected = max(len(plan) // 2, 1)
     return pl.pallas_call(
@@ -408,7 +406,13 @@
 
 
 def pair_tables(pair_list, per_device, devices):
-    pairs = lax.all_gather(pair_list, "img", axis=0, tiled=False)
+    pairs = lax.all_to_all(
+        jnp.broadcast_to(pair_list[None], (devices,) + pair_list.shape),
+        "img",
+        split_axis=0,
+        concat_axis=0,
+        tiled=True,
+    )
     listing = jnp.arange(devices, dtype=jnp.int32)
     first_local = pairs[:, :, 0] - listing[:, None] * per_device
     owner = pairs[:, :, 1] // per_device
@@ -416,7 +420,7 @@
     hit = owner[:, :, None] == listing[None, None, :]
     firsts = jnp.sum(jnp.where(hit, first_local[:, :, None] + 1, 0), axis=1)
     seconds = jnp.sum(jnp.where(hit, second_local[:, :, None] + 1, 0), axis=1)
-    return firsts, seconds
+    return pairs, firsts, seconds
 
 
 def always(me):
@@ -447,7 +451,7 @@
     return run_branches(branches, tables, devices, length, (fetched,), shared, None, tokens)
 
 
-def line_exchange(tokens, tables, devices, shared_of):
+def line_exchange(tokens, pairs, tables, devices, shared_of):
     length = tokens.shape[1]
     changes = range(1, PLANE)
     slots = range(SLOTS)
@@ -496,7 +500,7 @@
     def to_others(packed):
         return [across(packed[change - 1], 0, change) for change in changes]
 
-    tokens, *tables = pinned((tokens, *tables))
+    tokens, _ = pinned((tokens, pairs))
     up_one = hop(tokens, 1, (0, 1, 2))
     down_one = hop(tokens, -1, (1, 2, 3))
     packing = [
@@ -599,7 +603,7 @@
     per_device, length, feats = tokens.shape
     devices = lax.axis_size("img")
     me = lax.axis_index("img")
-    firsts, seconds = pair_tables(pair_list, per_device, devices)
+    pairs, firsts, seconds = pair_tables(pair_list, per_device, devices)
     tables = (firsts.reshape(-1), seconds.reshape(-1), me.astype(jnp.int32)[None])
 
     def shared_of():
@@ -615,7 +619,7 @@
         )
 
     if devices == 4 * PLANE:
-        merged = line_exchange(tokens, tables, devices, shared_of)
+        merged = line_exchange(tokens, pairs, tables, devices, shared_of)
     else:
         merged = dense_exchange(tokens, tables, devices, shared_of())
     merged = merged.reshape(length, feats // 128, per_device, 128)

time: 248 us -> 224 us (0.903)
  the two profiles are of different devices: /device:TPU:7 before, /device:TPU:1 now
where the time goes in v1:
time: 224 us; the launch traced here: 225 us
  Pallas kernels  109 us (49%)
  waiting for transfers between devices  45.5 us (20%)
  local copies, waits for them, and re-layouts  26.3 us (12%)
  starting transfers between devices  25.8 us (12%)
  blocking collectives  13 us (6%)
  other arithmetic  4.72 us (2%)
    pallas_call x4, Pallas kernels, run_branches(): pl.pallas_call(functools.partial(branch_kernel, plan, devices, len(partne...  88.1 us
    ppermute x14, waiting for transfers between devices, across(): lax.ppermute(array, 'img', [(p * PLANE + c, (p ^ flip) * PLANE + (c ^ cha...  24.5 us
    ppermute x4, waiting for transfers between devices, hop(): lax.ppermute(array, 'img', [(p * PLANE + c, (p + step) * PLANE + c) for p...  21.1 us
    ppermute x14, starting transfers between devices, across(): lax.ppermute(array, 'img', [(p * PLANE + c, (p ^ flip) * PLANE + (c ^ cha...  18.5 us
    all_to_all x1, blocking collectives, pair_tables(): lax.all_to_all(jnp.broadcast_to(pair_list[None], (devices,) + pair_list.s...  13 us
    pallas_call x4, Pallas kernels, pack(): pl.pallas_call(functools.partial(pack_kernel, plan, devices, len(sources)...  11.7 us
    unnamed x30, local copies, waits for them, and re-layouts  10.6 us
    pallas_call x1, Pallas kernels, prepare(): pl.pallas_call(prep_kernel, out_shape=(jax.ShapeDtypeStruct((images, feat...  9.53 us
  transfers between devices with their start and end apart: 18, of which 7 were waited for; matrix products, arithmetic and copies ran while one was open for 12% of the time, Pallas kernels for 39%

profile of v1, /device:TPU:1, one launch (start us, length us, event | category | flops | bytes accessed | tf_op | source)
XLA Modules:
  0.0 225.1 jit_solution(12615222536700800089)
XLA Ops:
  0.7 13.0 %all_to_all.5 = s32[16,8,2]{1,2,0:T(2,128)S(1)} all-to-all(s32[16,8,2]{1,2,0:T(2,128)S(1)} %broadcast_in_dim.51), channel_id=1, replica_groups=mesh['groups'=2,'img'=16] {'img'}, dimensions={0} | all-to-all | bytes 2048 | tf_op jit(solution)/shard_map/all_to_all | solution.py:409
  13.7 3.9 %collective-permute-start = (bf16[8,196,768]{2,0,1:T(8,128)(2,1)}, bf16[8,196,768]{2,0,1:T(8,128)(2,1)}, u32[]{:S(2)}, u32[]{:S(2)}) collective-permute-start(bf16[8,196,768]{2,0,1:T(8,128)(2,1)} %param.9), channel_id=1, source_target_pairs={{0,4},{1,5},{2,6},{3,7},{4,8},{5,9},{6,10},{7,11},{8,12},{9,13},{1... | collective-permute-start | bytes 7225352 | tf_op jit(solution)/shard_map/ppermute | solution.py:461
  18.9 3.6 %copy.49.refs_0_.refs_11_ = bf16[8,196,768]{2,1,0:T(8,128)(2,1)} copy(bf16[8,196,768]{2,0,1:T(8,128)(2,1)} %param.9) | data formatting | bytes 4816896 | tf_op jit(solution)/shard_map/optimization_barrier | solution.py:503
  24.3 2.8 %pack_images.4 = (bf16[400,768]{1,0:T(8,128)(2,1)}, bf16[400,768]{1,0:T(8,128)(2,1)}, bf16[400,768]{1,0:T(8,128)(2,1)}) custom-call(s32[256]{0:T(256)} %reshape.27.firsts_ref, s32[256]{0:T(256)} %reshape.28.seconds_ref, s32[1]{0:T(128)} %bitcast.3.me_ref, bf16[8,196,768]{2,1,0:T(8,128)(2,1)} %copy.49.refs_0_.refs_11_), custom_call_target="tpu_custom_call" | custom-call | tf_op jit(solution)/shard_map/pack_images/pallas_call | solution.py:317
  32.2 2.5 %copy.50 = bf16[768,768]{0,1:T(8,128)(2,1)} copy(bf16[768,768]{1,0:T(8,128)(2,1)} %param.11) | data formatting | bytes 2359296 | tf_op args[2]
  40.3 9.5 %own_queries.1 = (bf16[8,768,256]{2,1,0:T(8,128)(2,1)}, f32[8,1,256]{2,1,0:T(1,128)}) custom-call(bf16[8,196,768]{2,1,0:T(8,128)(2,1)} %copy.51.tokens_ref, bf16[768,768]{1,0:T(8,128)(2,1)} %bitcast.23, f32[1,768]{1,0:T(1,128)} %broadcast_in_dim.58.gain_ref, f32[1,768]{1,0:T(1,128)} %broadcast_in_dim.59.conf_row_ref), custom_call_target="tpu_custom_call" | custom-call | tf_op jit(solution)/shard_map/own_queries/pallas_call | solution.py:394
  49.8 8.1 %collective-permute-done.4.refs_3_ = bf16[400,768]{1,0:T(8,128)(2,1)} collective-permute-done((bf16[400,768]{1,0:T(8,128)(2,1)}, bf16[400,768]{1,0:T(8,128)(2,1)}, u32[]{:S(2)}, u32[]{:S(2)}) %collective-permute-start.4) | collective-permute-done | bytes 614432 | tf_op jit(solution)/shard_map/ppermute | solution.py:468
  57.9 9.8 %collective-permute-done = bf16[8,196,768]{2,0,1:T(8,128)(2,1)} collective-permute-done((bf16[8,196,768]{2,0,1:T(8,128)(2,1)}, bf16[8,196,768]{2,0,1:T(8,128)(2,1)}, u32[]{:S(2)}, u32[]{:S(2)}) %collective-permute-start) | collective-permute-done | bytes 2408480 | tf_op jit(solution)/shard_map/ppermute | solution.py:461
  67.7 5.3 %collective-permute-done.1 = bf16[8,196,768]{2,0,1:T(8,128)(2,1)} collective-permute-done((bf16[8,196,768]{2,0,1:T(8,128)(2,1)}, bf16[8,196,768]{2,0,1:T(8,128)(2,1)}, u32[]{:S(2)}, u32[]{:S(2)}) %collective-permute-start.1) | collective-permute-done | bytes 2408480 | tf_op jit(solution)/shard_map/ppermute | solution.py:461
  76.0 3.6 %copy.55.refs_1_.refs_0_ = bf16[8,196,768]{2,1,0:T(8,128)(2,1)} copy(bf16[8,196,768]{2,0,1:T(8,128)(2,1)} %collective-permute-done) | data formatting | bytes 4816896 | tf_op jit(solution)/shard_map/optimization_barrier | solution.py:513
  79.5 3.6 %copy.56.refs_2_.refs_1_ = bf16[8,196,768]{2,1,0:T(8,128)(2,1)} copy(bf16[8,196,768]{2,0,1:T(8,128)(2,1)} %collective-permute-done.1) | data formatting | bytes 4816896 | tf_op jit(solution)/shard_map/optimization_barrier | solution.py:513
  83.1 3.2 %pack_images.5 = (bf16[400,768]{1,0:T(8,128)(2,1)}, bf16[400,768]{1,0:T(8,128)(2,1)}, bf16[400,768]{1,0:T(8,128)(2,1)}, bf16[400,768]{1,0:T(8,128)(2,1)}, bf16[4...) custom-call(s32[256]{0:T(256)} %reshape.27.firsts_ref, s32[256]{0:T(256)} %reshape.28.seconds_ref, s32[1]{0:T(128)} %bitcast.3.me_ref, ...), custom_call_target="tpu_custom_call" | custom-call | tf_op jit(solution)/shard_map/pack_images/pallas_call | solution.py:317
  90.4 20.0 %attend_branches.4 = (f32[8,768,256]{2,1,0:T(8,128)}, f32[8,1,256]{2,1,0:T(1,128)}) custom-call(s32[256]{0:T(256)} %reshape.27.firsts_ref, s32[256]{0:T(256)} %reshape.28.seconds_ref, s32[1]{0:T(128)} %bitcast.3.me_ref, bf16[8,196,768]{2,1,0:T(8,128)(2,1)} %copy.49.refs_0_.refs_11_, bf16[400,768]{1,0:T(8,128)(2,1)} %copy-done.8, ...), custom_call_target="tpu_custom_call" | custom-call | flops 5200000000 | bytes 8000000 | tf_op jit(solution)/shard_map/attend_branches/pallas_call | solution.py:375
  110.4 7.7 %collective-permute-done.9.refs_3_.refs_7_ = bf16[400,768]{1,0:T(8,128)(2,1)} collective-permute-done((bf16[400,768]{1,0:T(8,128)(2,1)}, bf16[400,768]{1,0:T(8,128)(2,1)}, u32[]{:S(2)}, u32[]{:S(2)}) %collective-permute-start.9) | collective-permute-done | bytes 614432 | tf_op jit(solution)/shard_map/ppermute | solution.py:468
  120.2 2.9 %pack_images.6 = (bf16[800,768]{1,0:T(8,128)(2,1)}, bf16[800,768]{1,0:T(8,128)(2,1)}) custom-call(s32[256]{0:T(256)} %reshape.27.firsts_ref, s32[256]{0:T(256)} %reshape.28.seconds_ref, s32[1]{0:T(128)} %bitcast.3.me_ref, bf16[8,196,768]{2,1,0:T(8,128)(2,1)} %copy.49.refs_0_.refs_11_, bf16[400,768]{1,0:T(8,128)(2,1)} %copy-done.4, ...), custom_call_target="tpu_custom_call" | custom-call | tf_op jit(solution)/shard_map/pack_images/pallas_call | solution.py:317
  123.1 6.1 %collective-permute-done.6 = bf16[8,196,768]{2,0,1:T(8,128)(2,1)} collective-permute-done((bf16[8,196,768]{2,0,1:T(8,128)(2,1)}, bf16[8,196,768]{2,0,1:T(8,128)(2,1)}, u32[]{:S(2)}, u32[]{:S(2)}) %collective-permute-start.6) | collective-permute-done | bytes 2408480 | tf_op jit(solution)/shard_map/ppermute | solution.py:461
  131.0 5.2 %collective-permute-start.11 = (bf16[800,768]{1,0:T(8,128)(2,1)}, bf16[800,768]{1,0:T(8,128)(2,1)S(1)}, u32[]{:S(2)}, u32[]{:S(2)}) collective-permute-start(bf16[800,768]{1,0:T(8,128)(2,1)} %get-tuple-element.110), channel_id=1, source_target_pairs={{0,12},{1,13},{2,14},{3,15},{12,0},{13,1},{14,2},{15,3},{16,28},{1... | collective-permute-start | bytes 3686408 | tf_op jit(solution)/shard_map/ppermute | solution.py:468
  136.2 4.6 %copy_select_fusion.refs_0_ = bf16[8,196,768]{2,1,0:T(8,128)(2,1)} fusion(bf16[8,196,768]{2,0,1:T(8,128)(2,1)S(1)} %collective-permute-done.5, bf16[8,196,768]{2,0,1:T(8,128)(2,1)} %collective-permute-done.6, pred[]{:T(512)S(6)} %lt.3), kind=kLoop, calls=%fused_computation | loop fusion | flops 1204224 | bytes 7225345 | tf_op jit(solution)/shard_map/jit(_where)/select_n | solution.py:555
  140.8 2.8 %pack_images.7 = (bf16[400,768]{1,0:T(8,128)(2,1)}, bf16[400,768]{1,0:T(8,128)(2,1)}, bf16[400,768]{1,0:T(8,128)(2,1)}) custom-call(s32[256]{0:T(256)} %reshape.27.firsts_ref, s32[256]{0:T(256)} %reshape.28.seconds_ref, s32[1]{0:T(128)} %bitcast.3.me_ref, bf16[8,196,768]{2,1,0:T(8,128)(2,1)} %copy_select_fusion.refs_0_), custom_call_target="tpu_custom_call" | custom-call | tf_op jit(solution)/shard_map/pack_images/pallas_call | solution.py:317
  143.6 3.7 %collective-permute-done.14.refs_4_ = bf16[400,768]{1,0:T(8,128)(2,1)} collective-permute-done((bf16[400,768]{1,0:T(8,128)(2,1)}, bf16[400,768]{1,0:T(8,128)(2,1)}, u32[]{:S(2)}, u32[]{:S(2)}) %collective-permute-start.14) | collective-permute-done | bytes 614432 | tf_op jit(solution)/shard_map/ppermute | solution.py:468
  149.4 22.1 %attend_branches.5 = (f32[8,768,256]{2,1,0:T(8,128)}, f32[8,1,256]{2,1,0:T(1,128)}) custom-call(s32[256]{0:T(256)} %reshape.27.firsts_ref, s32[256]{0:T(256)} %reshape.28.seconds_ref, s32[1]{0:T(128)} %bitcast.3.me_ref, bf16[8,196,768]{2,1,0:T(8,128)(2,1)} %copy.55.refs_1_.refs_0_, bf16[8,196,768]{2,1,0:T(8,128)(2,1)} %copy.56.refs_2_.refs_1_, ...), custom_call_target="tpu_custom_call" | custom-call | flops 10400000000 | bytes 16000000 | tf_op jit(solution)/shard_map/attend_branches/pallas_call | solution.py:375
  171.6 5.0 %collective-permute-done.17.refs_3_ = bf16[400,768]{1,0:T(8,128)(2,1)S(1)} collective-permute-done((bf16[400,768]{1,0:T(8,128)(2,1)}, bf16[400,768]{1,0:T(8,128)(2,1)S(1)}, u32[]{:S(2)}, u32[]{:S(2)}) %collective-permute-start.17) | collective-permute-done | bytes 614432 | tf_op jit(solution)/shard_map/ppermute | solution.py:468
  177.4 24.2 %attend_branches.6 = (f32[8,768,256]{2,1,0:T(8,128)}, f32[8,1,256]{2,1,0:T(1,128)}) custom-call(s32[256]{0:T(256)} %reshape.27.firsts_ref, s32[256]{0:T(256)} %reshape.28.seconds_ref, s32[1]{0:T(128)} %bitcast.3.me_ref, bf16[8,196,768]{2,1,0:T(8,128)(2,1)} %copy_select_fusion.refs_0_, bf16[400,768]{1,0:T(8,128)(2,1)} %copy-done.9, ...), custom_call_target="tpu_custom_call" | custom-call | flops 5200000000 | bytes 8000000 | tf_op jit(solution)/shard_map/attend_branches/pallas_call | solution.py:375
  203.1 21.9 %attend_branches.7 = f32[9408,128]{1,0:T(8,128)} custom-call(s32[256]{0:T(256)} %reshape.27.firsts_ref, s32[256]{0:T(256)} %reshape.28.seconds_ref, s32[1]{0:T(128)} %bitcast.3.me_ref, bf16[800,768]{1,0:T(8,128)(2,1)} %copy-done.1, bf16[800,768]{1,0:T(8,128)(2,1)} %copy-done.2, f32[8,1,256]{2,1,0:T(1,128)} %get-tuple-element.95.refs_4_.refs_8_.refs_2_, ...), custom_call_target="tpu_custom_call" | custom-call | flops 5200000000 | bytes 8000000 | tf_op jit(solution)/shard_map/attend_branches/pallas_call | solution.py:375
  (71 shorter events, 30.0 us)
Async XLA Ops:
  13.7 54.0 %collective-permute-start = (bf16[8,196,768]{2,0,1:T(8,128)(2,1)}, bf16[8,196,768]{2,0,1:T(8,128)(2,1)}, u32[]{:S(2)}, u32[]{:S(2)}) collective-permute-start(bf16[8,196,768]{2,0,1:T(8,128)(2,1)} %param.9), channel_id=1, source_target_pairs={{0,4},{1,5},{2,6},{3,7},{4,8},{5,9},{6,10},{7,11},{8,12},{9,13},{1... | collective-permute-start | bytes 7225352 | tf_op jit(solution)/shard_map/ppermute | solution.py:461
  17.6 55.4 %collective-permute-start.1 = (bf16[8,196,768]{2,0,1:T(8,128)(2,1)}, bf16[8,196,768]{2,0,1:T(8,128)(2,1)}, u32[]{:S(2)}, u32[]{:S(2)}) collective-permute-start(bf16[8,196,768]{2,0,1:T(8,128)(2,1)} %param.9), channel_id=1, source_target_pairs={{4,0},{5,1},{6,2},{7,3},{8,4},{9,5},{10,6},{11,7},{12,8},{13,9},{1... | collective-permute-start | bytes 7225352 | tf_op jit(solution)/shard_map/ppermute | solution.py:461
  22.5 7.8 %copy-start = (bf16[8,196,768]{2,0,1:T(8,128)(2,1)S(1)}, bf16[8,196,768]{2,0,1:T(8,128)(2,1)}, u32[]{:S(2)}) copy-start(bf16[8,196,768]{2,0,1:T(8,128)(2,1)} %param.9) | copy-start | bytes 7225348
  27.2 22.6 %collective-permute-start.2 = (bf16[400,768]{1,0:T(8,128)(2,1)}, bf16[400,768]{1,0:T(8,128)(2,1)S(1)}, u32[]{:S(2)}, u32[]{:S(2)}) collective-permute-start(bf16[400,768]{1,0:T(8,128)(2,1)} %get-tuple-element.69), channel_id=1, source_target_pairs={{0,1},{1,0},{2,3},{3,2},{4,5},{5,4},{6,7},{7,6},{8,9},{9,8},{10,11... | collective-permute-start | bytes 1843208 | tf_op jit(solution)/shard_map/ppermute | solution.py:468
  28.6 21.2 %collective-permute-start.3 = (bf16[400,768]{1,0:T(8,128)(2,1)}, bf16[400,768]{1,0:T(8,128)(2,1)}, u32[]{:S(2)}, u32[]{:S(2)}) collective-permute-start(bf16[400,768]{1,0:T(8,128)(2,1)} %get-tuple-element.70), channel_id=1, source_target_pairs={{0,2},{1,3},{2,0},{3,1},{4,6},{5,7},{6,4},{7,5},{8,10},{9,11},{10,... | collective-permute-start | bytes 1843208 | tf_op jit(solution)/shard_map/ppermute | solution.py:468
  28.8 6.5 %copy-start.5 = (f32[768]{0:T(1024)S(1)}, f32[768]{0:T(1024)}, u32[]{:S(2)}) copy-start(f32[768]{0:T(1024)} %param.17) | copy-start | bytes 9220
  28.8 7.1 %copy-start.7 = (f32[768]{0:T(1024)S(1)}, f32[768]{0:T(1024)}, u32[]{:S(2)}) copy-start(f32[768]{0:T(1024)} %param.16) | copy-start | bytes 9220
  28.8 29.2 %collective-permute-start.4 = (bf16[400,768]{1,0:T(8,128)(2,1)}, bf16[400,768]{1,0:T(8,128)(2,1)}, u32[]{:S(2)}, u32[]{:S(2)}) collective-permute-start(bf16[400,768]{1,0:T(8,128)(2,1)} %get-tuple-element.71), channel_id=1, source_target_pairs={{0,3},{1,2},{2,1},{3,0},{4,7},{5,6},{6,5},{7,4},{8,11},{9,10},{10,... | collective-permute-start | bytes 1843208 | tf_op jit(solution)/shard_map/ppermute | solution.py:468
  32.2 6.7 %copy-start.3 = (bf16[768,768]{1,0:T(8,128)(2,1)S(1)}, bf16[768,768]{1,0:T(8,128)(2,1)}, u32[]{:S(2)}) copy-start(bf16[768,768]{1,0:T(8,128)(2,1)} %param.14) | copy-start | bytes 3538948
  49.8 29.8 %copy-start.8 = (bf16[400,768]{1,0:T(8,128)(2,1)}, bf16[400,768]{1,0:T(8,128)(2,1)S(1)}, u32[]{:S(2)}) copy-start(bf16[400,768]{1,0:T(8,128)(2,1)S(1)} %collective-permute-done.2.refs_1_) | copy-start | bytes 1843204
  73.9 49.2 %collective-permute-start.5 = (bf16[8,196,768]{2,0,1:T(8,128)(2,1)}, bf16[8,196,768]{2,0,1:T(8,128)(2,1)S(1)}, u32[]{:S(2)}, u32[]{:S(2)}) collective-permute-start(bf16[8,196,768]{2,0,1:T(8,128)(2,1)} %collective-permute-done), channel_id=1, source_target_pairs={{4,8},{5,9},{6,10},{7,11},{8,12},{9,13},{10,14},{11,15},{20,24},{2... | collective-permute-start | bytes 7225352 | tf_op jit(solution)/shard_map/ppermute | solution.py:461
  74.7 54.5 %collective-permute-start.6 = (bf16[8,196,768]{2,0,1:T(8,128)(2,1)}, bf16[8,196,768]{2,0,1:T(8,128)(2,1)}, u32[]{:S(2)}, u32[]{:S(2)}) collective-permute-start(bf16[8,196,768]{2,0,1:T(8,128)(2,1)} %collective-permute-done.1), channel_id=1, source_target_pairs={{4,0},{5,1},{6,2},{7,3},{8,4},{9,5},{10,6},{11,7},{20,16},{21,17},... | collective-permute-start | bytes 7225352 | tf_op jit(solution)/shard_map/ppermute | solution.py:461
  86.3 24.0 %collective-permute-start.7 = (bf16[400,768]{1,0:T(8,128)(2,1)}, bf16[400,768]{1,0:T(8,128)(2,1)S(1)}, u32[]{:S(2)}, u32[]{:S(2)}) collective-permute-start(bf16[400,768]{1,0:T(8,128)(2,1)} %get-tuple-element.83), channel_id=1, source_target_pairs={{0,1},{1,0},{2,3},{3,2},{4,5},{5,4},{6,7},{7,6},{8,9},{9,8},{10,11... | collective-permute-start | bytes 1843208 | tf_op jit(solution)/shard_map/ppermute | solution.py:468
  88.7 21.7 %collective-permute-start.8 = (bf16[400,768]{1,0:T(8,128)(2,1)}, bf16[400,768]{1,0:T(8,128)(2,1)}, u32[]{:S(2)}, u32[]{:S(2)}) collective-permute-start(bf16[400,768]{1,0:T(8,128)(2,1)} %get-tuple-element.84), channel_id=1, source_target_pairs={{0,2},{1,3},{2,0},{3,1},{4,6},{5,7},{6,4},{7,5},{8,10},{9,11},{10,... | collective-permute-start | bytes 1843208 | tf_op jit(solution)/shard_map/ppermute | solution.py:468
  88.7 29.3 %collective-permute-start.9 = (bf16[400,768]{1,0:T(8,128)(2,1)}, bf16[400,768]{1,0:T(8,128)(2,1)}, u32[]{:S(2)}, u32[]{:S(2)}) collective-permute-start(bf16[400,768]{1,0:T(8,128)(2,1)} %get-tuple-element.85), channel_id=1, source_target_pairs={{0,3},{1,2},{2,1},{3,0},{4,7},{5,6},{6,5},{7,4},{8,11},{9,10},{10,... | collective-permute-start | bytes 1843208 | tf_op jit(solution)/shard_map/ppermute | solution.py:468
  110.3 9.8 %copy-start.4 = (bf16[400,768]{1,0:T(8,128)(2,1)}, bf16[400,768]{1,0:T(8,128)(2,1)S(1)}, u32[]{:S(2)}) copy-start(bf16[400,768]{1,0:T(8,128)(2,1)S(1)} %collective-permute-done.7.refs_1_.refs_5_) | copy-start | bytes 1843204
  118.0 25.6 %collective-permute-start.12 = (bf16[400,768]{1,0:T(8,128)(2,1)}, bf16[400,768]{1,0:T(8,128)(2,1)}, u32[]{:S(2)}, u32[]{:S(2)}) collective-permute-start(bf16[400,768]{1,0:T(8,128)(2,1)} %get-tuple-element.116), channel_id=1, source_target_pairs={{0,1},{1,0},{2,3},{3,2},{4,5},{5,4},{6,7},{7,6},{8,9},{9,8},{10,11... | collective-permute-start | bytes 1843208 | tf_op jit(solution)/shard_map/ppermute | solution.py:468
  118.0 25.6 %collective-permute-start.13 = (bf16[400,768]{1,0:T(8,128)(2,1)}, bf16[400,768]{1,0:T(8,128)(2,1)}, u32[]{:S(2)}, u32[]{:S(2)}) collective-permute-start(bf16[400,768]{1,0:T(8,128)(2,1)} %get-tuple-element.117), channel_id=1, source_target_pairs={{0,2},{1,3},{2,0},{3,1},{4,6},{5,7},{6,4},{7,5},{8,10},{9,11},{10,... | collective-permute-start | bytes 1843208 | tf_op jit(solution)/shard_map/ppermute | solution.py:468
  118.1 29.2 %collective-permute-start.14 = (bf16[400,768]{1,0:T(8,128)(2,1)}, bf16[400,768]{1,0:T(8,128)(2,1)}, u32[]{:S(2)}, u32[]{:S(2)}) collective-permute-start(bf16[400,768]{1,0:T(8,128)(2,1)} %get-tuple-element.118), channel_id=1, source_target_pairs={{0,3},{1,2},{2,1},{3,0},{4,7},{5,6},{6,5},{7,4},{8,11},{9,10},{10,... | collective-permute-start | bytes 1843208 | tf_op jit(solution)/shard_map/ppermute | solution.py:468
  129.1 72.4 %collective-permute-start.10 = (bf16[800,768]{1,0:T(8,128)(2,1)}, bf16[800,768]{1,0:T(8,128)(2,1)S(1)}, u32[]{:S(2)}, u32[]{:S(2)}) collective-permute-start(bf16[800,768]{1,0:T(8,128)(2,1)} %get-tuple-element.109), channel_id=1, source_target_pairs={{0,12},{1,13},{2,14},{3,15},{12,0},{13,1},{14,2},{15,3},{16,28},{1... | collective-permute-start | bytes 3686408 | tf_op jit(solution)/shard_map/ppermute | solution.py:468
  131.0 70.6 %collective-permute-start.11 = (bf16[800,768]{1,0:T(8,128)(2,1)}, bf16[800,768]{1,0:T(8,128)(2,1)S(1)}, u32[]{:S(2)}, u32[]{:S(2)}) collective-permute-start(bf16[800,768]{1,0:T(8,128)(2,1)} %get-tuple-element.110), channel_id=1, source_target_pairs={{0,12},{1,13},{2,14},{3,15},{12,0},{13,1},{14,2},{15,3},{16,28},{1... | collective-permute-start | bytes 3686408 | tf_op jit(solution)/shard_map/ppermute | solution.py:468
  147.3 24.2 %collective-permute-start.15 = (bf16[400,768]{1,0:T(8,128)(2,1)}, bf16[400,768]{1,0:T(8,128)(2,1)S(1)}, u32[]{:S(2)}, u32[]{:S(2)}) collective-permute-start(bf16[400,768]{1,0:T(8,128)(2,1)} %get-tuple-element.119), channel_id=1, source_target_pairs={{0,1},{1,0},{2,3},{3,2},{4,5},{5,4},{6,7},{7,6},{8,9},{9,8},{10,11... | collective-permute-start | bytes 1843208 | tf_op jit(solution)/shard_map/ppermute | solution.py:468
  147.3 24.2 %collective-permute-start.16 = (bf16[400,768]{1,0:T(8,128)(2,1)}, bf16[400,768]{1,0:T(8,128)(2,1)S(1)}, u32[]{:S(2)}, u32[]{:S(2)}) collective-permute-start(bf16[400,768]{1,0:T(8,128)(2,1)} %get-tuple-element.120), channel_id=1, source_target_pairs={{0,2},{1,3},{2,0},{3,1},{4,6},{5,7},{6,4},{7,5},{8,10},{9,11},{10,... | collective-permute-start | bytes 1843208 | tf_op jit(solution)/shard_map/ppermute | solution.py:468
  147.4 29.2 %collective-permute-start.17 = (bf16[400,768]{1,0:T(8,128)(2,1)}, bf16[400,768]{1,0:T(8,128)(2,1)S(1)}, u32[]{:S(2)}, u32[]{:S(2)}) collective-permute-start(bf16[400,768]{1,0:T(8,128)(2,1)} %get-tuple-element.121), channel_id=1, source_target_pairs={{0,3},{1,2},{2,1},{3,0},{4,7},{5,6},{6,5},{7,4},{8,11},{9,10},{10,... | collective-permute-start | bytes 1843208 | tf_op jit(solution)/shard_map/ppermute | solution.py:468
  (6 other events, 19.3 us)
